TPU v7x, 32 devices: a whole 2x2x4 slice. The times are simulated.
32 devices in a mesh: groups: 2 (over x), dp: 4 (over y, core), layer: 4 (over z).
Axes of the slice: x: 2, y: 2, z: 4, core: 2. Of those that a mesh axis runs over, the one named last changes fastest.
Arguments:
- activations: bfloat16 [4, 4096, 8192], P('layer', ('groups', 'dp')), parts along dimension 1, may hold values from -6 to 6
- gradients: bfloat16 [4, 4096, 4096], P('layer', ('groups', 'dp')), parts along dimension 1, may hold values from -6 to 6
- left_factors: bfloat16 [4, 512, 8192], P('layer', ('groups', 'dp')), parts along dimension 1, may hold values from -0.0625 to 0.0625
- right_factors: bfloat16 [4, 512, 4096], P('layer', ('groups', 'dp')), parts along dimension 1, may hold values from -0.09375 to 0.09375
- lengths: int32 [32], P(('groups', 'dp')), parts along dimension 0, may hold values from 1 to 256, as said below
- segment_ids: int32 [4096], P(('groups', 'dp')), parts along dimension 0, may hold values from 0 to 4, as said below
Outputs:
- scores: float32 [32, 8], P(('groups', 'dp'), 'layer'), parts along dimension 0
There are 2 independent parts, one for each index of `groups`. A program takes and returns all parts, laid end to end along the dimension named above; each array names one. Nothing has to cross between parts.
Inputs may be any that keep to these rules, and one draw needn't show every extreme that they name: Within each dp shard the 4 lengths add up to less than 512, and exactly one of them is 256. `segment_ids`: within each dp shard of 512 slots the ids never fall, id g fills exactly lengths of that shard's sequence g, and the last slots, at least one, hold 4 (padding).
All inputs are finite; a program needn't handle non-finite values.
Results may differ from a plain program's by a relative error of at most 0.0003.
Values may be sent and summed in bfloat16 or wider, within the bound.
A program may use at most 128 MiB of HBM per device.

v0:
```python
import jax
import jax.numpy as jnp
from jax import lax
from jax.sharding import PartitionSpec as P

RANK = 32


def local(activations, gradients, left_factors, right_factors, lengths, segment_ids):
    seq_count = lengths.shape[0]
    tok_count = segment_ids.shape[0]
    member_mask = (segment_ids[None, :] == jnp.arange(seq_count, dtype=jnp.int32)[:, None]).astype(
        jnp.float32
    )
    left_piece = lax.all_gather(left_factors, "dp", axis=1, tiled=True)
    row_count = left_piece.shape[1]
    proj_left = lax.dot_general(
        activations[0], left_piece[0], (((1,), (1,)), ((), ())), preferred_element_type=jnp.float32
    )
    proj_right = lax.dot_general(
        gradients[0],
        lax.all_gather(right_factors, "dp", axis=1, tiled=True)[0],
        (((1,), (1,)), ((), ())),
        preferred_element_type=jnp.float32,
    )
    per_token = jnp.sum(
        (proj_left * proj_right).reshape(tok_count, row_count // RANK, RANK), axis=-1
    )
    summed = jnp.dot(
        member_mask, per_token, precision=lax.Precision.HIGHEST, preferred_element_type=jnp.float32
    )
    summed_scores = lax.psum_scatter(summed, "layer", scatter_dimension=1, tiled=True)
    return summed_scores / lengths.astype(jnp.float32)[:, None]


def solution(mesh):
    return jax.shard_map(
        local,
        mesh=mesh,
        in_specs=(
            P("layer", ("groups", "dp"), None),
            P("layer", ("groups", "dp"), None),
            P("layer", ("groups", "dp"), None),
            P("layer", ("groups", "dp"), None),
            P(("groups", "dp")),
            P(("groups", "dp")),
        ),
        out_specs=P(("groups", "dp"), "layer"),
        check_vma=False,
    )
```

profile of v0, /device:TPU:0, one launch (start us, length us, event | category | flops | bytes accessed | tf_op | source)
XLA Modules:
  0.0 93.7 jit_solution(11562484582080511695)
XLA Ops:
  6.5 0.0 all-gather.3.cloned.1.call-start
  6.5 0.7 all-gather.3.cloned.1.call-update
  7.3 0.0 all-gather.5.cloned.1.call-start
  7.3 0.7 all-gather.5.cloned.1.call-update
  8.0 0.7 convert_element_type.4
  8.7 1.2 %dynamic-slice = u32[1]{0:T(128)} dynamic-slice(u32[32]{0:T(128)} %constant.9, u32[]{:T(128)S(6)} %add.3), dynamic_slice_sizes={1} | dynamic-slice | bytes 12
  10.6 35.6 %all-gather.3.cloned.1.call-done = bf16[1,256,8192]{2,1,0:T(8,128)(2,1)} async-done(((bf16[1,64,8192]{2,1,0:T(8,128)(2,1)}), bf16[1,256,8192]{2,1,0:T(8,128)(2,1)}) %all-gather.3.cloned.1.call-update) | async-done | bytes 4194320 | tf_op jit(solution)/shard_map/all_gather | solution.py:15
  46.1 6.9 %fusion = f32[512,256]{0,1:T(8,128)S(1)} fusion(bf16[1,512,8192]{2,1,0:T(8,128)(2,1)} %param.6, bf16[1,256,8192]{2,1,0:T(8,128)(2,1)} %all-gather.3.cloned.1.call-done), kind=kOutput, calls=%fused_computation | convolution fusion | flops 2147483648 | bytes 13107200 | tf_op jit(solution)/shard_map/dot_general | solution.py:17
  53.1 0.0 copy-start
  53.1 17.2 %all-gather.5.cloned.1.call-done = bf16[1,256,4096]{2,1,0:T(8,128)(2,1)} async-done(((bf16[1,64,4096]{2,1,0:T(8,128)(2,1)}), bf16[1,256,4096]{2,1,0:T(8,128)(2,1)}) %all-gather.5.cloned.1.call-update) | async-done | bytes 2097168 | tf_op jit(solution)/shard_map/all_gather | solution.py:22
  70.3 4.2 %bitcast_reduce_fusion = f32[512,8]{0,1:T(8,128)S(1)} fusion(f32[512,256]{0,1:T(8,128)S(1)} %fusion, bf16[1,256,4096]{2,1,0:T(8,128)(2,1)} %all-gather.5.cloned.1.call-done, bf16[1,512,4096]{2,1,0:T(8,128)(2,1)} %param.7), kind=kOutput, calls=%fused_computation.7 | convolution fusion | flops 1073999872 | bytes 6832128 | tf_op jit(solution)/shard_map/dot_general | solution.py:20
  74.5 0.0 copy-done
  74.5 0.1 fusion.11
  74.6 11.7 %all-reduce = f32[4,8]{0,1:T(8,128)S(1)} all-reduce(f32[4,8]{0,1:T(8,128)S(1)} %fusion.11), channel_id=2, replica_groups=mesh['groups'=2,'dp'=4,'layer'=4] {'layer'}, use_global_device_ids=true, to_apply=%region_1.0.clone | all-reduce | flops 32 | bytes 256
  86.3 0.6 dynamic-slice_divide_fusion
Async XLA Ops:
  6.5 39.6 %all-gather.3.cloned.1.call-start = ((), (), s32[]{:S(2)}) async-start(), calls=%async_computation | async-start | bytes 5242880 | tf_op jit(solution)/shard_map/all_gather | solution.py:15
  7.3 63.1 %all-gather.5.cloned.1.call-start = ((), (), s32[]{:S(2)}) async-start(), calls=%async_computation.1 | async-start | bytes 2621440 | tf_op jit(solution)/shard_map/all_gather | solution.py:22
  53.1 21.4 %copy-start = (s32[512]{0:T(512)S(1)}, s32[512]{0:T(512)}, u32[]{:S(2)}) copy-start(s32[512]{0:T(512)} %param.11) | copy-start | bytes 6148
Sparse Core Ops, SparseCore 0:
  8.9 37.1 all-gather.2
  47.7 22.5 all-gather.4
where the time goes:
time: 93.9 us; the launch traced here: 93.7 us
  waiting for transfers between devices  54.2 us (58%)
  between operations  14.1 us (15%)
  blocking collectives  11.7 us (12%)
  matrix products  11.2 us (12%)
  local copies, waits for them, and re-layouts  1.24 us (1%)
  other arithmetic  1.23 us (1%)
    all_gather x1, waiting for transfers between devices, local(): left_piece = lax.all_gather(left_factors, 'dp', axis=1, tiled=True)  35.6 us
    all_gather x1, waiting for transfers between devices, local(): lax.all_gather(right_factors, 'dp', axis=1, tiled=True)[0]  17.2 us
    unnamed x1, blocking collectives  11.7 us
    dot_general x1, matrix products, local(): lax.dot_general(activations[0], left_piece[0], (((1,), (1,)), ((), ())),...  6.93 us
    dot_general x1, matrix products, local(): lax.dot_general(gradients[0], lax.all_gather(right_factors, 'dp', axis=1,...  4.16 us
  transfers between devices with their start and end apart: 2, of which 2 were waited for; matrix products, arithmetic and copies ran while one was open for 9% of the time, Pallas kernels for 0%

commit v1 on v0

v1 whole, which is shorter than its diff:
```python
import functools

import jax
import jax.numpy as jnp
from jax import lax
from jax.experimental import pallas as pl
from jax.experimental.pallas import tpu as pltpu
from jax.sharding import PartitionSpec as P

RANK = 32
LANES = 128
SUBLANES = 8
CHUNK = 512
WINDOW = 0
MESH = pl.DeviceIdType.MESH


def chunks_of(inner, width, chunk):
    left = [(0, k, chunk) for k in range(0, inner, chunk)]
    right = [(1, k, chunk) for k in range(0, width, chunk)]
    return left + right


def kernel(
    chunks, layers, chips, query_lanes,
    act, grad, left, right, seg,
    out,
    act_v, grad_v, left_v, right_v, seg_v, acc, part, inbox,
    load_sem, near_send, near_recv, cross_send, cross_recv, pass_send, pass_recv,
    sum_send, sum_recv,
):
    rows = left.shape[1]
    dp, layer = lax.axis_index("dp"), lax.axis_index("layer")
    chip, core = lax.div(dp, 2), lax.rem(dp, 2)
    sibling = {"dp": chip * 2 + 1 - core}
    mine = pl.ds(pl.multiple_of(core * rows, rows), rows)
    own, held = (left, right), (left_v, right_v)
    tokens = (act_v, grad_v)

    partners = [{"dp": lax.rem(chip + s, chips) * 2 + core} for s in range(1, chips)]
    origins = [lax.rem(chip + chips - s, chips) for s in range(1, chips)]
    others = [{"layer": lax.rem(layer + d, layers)} for d in range(1, layers)]

    barrier = pltpu.get_barrier_semaphore()
    peers = [sibling] + partners + others
    for peer in peers:
        pl.semaphore_signal(barrier, inc=1, device_id=peer, device_id_type=MESH)

    loads = [
        pltpu.make_async_copy(left.at[0], left_v.at[chip, mine], load_sem.at[0]),
        pltpu.make_async_copy(right.at[0], right_v.at[chip, mine], load_sem.at[1]),
        pltpu.make_async_copy(act.at[0], act_v, load_sem.at[2]),
        pltpu.make_async_copy(grad.at[0], grad_v, load_sem.at[3]),
        pltpu.make_async_copy(seg, seg_v, load_sem.at[4]),
    ]
    for load in loads:
        load.start()
    pl.semaphore_wait(barrier, len(peers))

    def cross_copy(s, i):
        side, k, size = chunks[i]
        return pltpu.make_async_remote_copy(
            src_ref=own[side].at[0, :, pl.ds(k, size)],
            dst_ref=held[side].at[chip, mine, pl.ds(k, size)],
            send_sem=cross_send.at[s, i], recv_sem=cross_recv.at[s, i],
            device_id=partners[s], device_id_type=MESH,
        )

    def pass_copy(s, i):
        side, k, size = chunks[i]
        block = held[side].at[origins[s], mine, pl.ds(k, size)]
        return pltpu.make_async_remote_copy(
            src_ref=block, dst_ref=block,
            send_sem=pass_send.at[s, i], recv_sem=pass_recv.at[s, i],
            device_id=sibling, device_id_type=MESH,
        )

    def near_copy(side):
        return pltpu.make_async_remote_copy(
            src_ref=own[side].at[0], dst_ref=held[side].at[chip, mine],
            send_sem=near_send.at[side], recv_sem=near_recv.at[side],
            device_id=sibling, device_id_type=MESH,
        )

    steps = [(s, i) for s in range(chips - 1) for i in range(len(chunks))]
    crossing = [cross_copy(s, i) for s, i in steps]
    passing = [pass_copy(s, i) for s, i in steps]
    near = [near_copy(0), near_copy(1)]
    ahead = WINDOW if WINDOW and chips == 2 else len(steps)
    for copy in crossing[:ahead]:
        copy.start()
    for copy in near:
        copy.start()

    def project(slot, source, i):
        side, k, size = chunks[i]
        product = lax.dot_general(
            tokens[side][:, k:k + size], held[side][source, :, k:k + size],
            (((1,), (1,)), ((), ())), preferred_element_type=jnp.float32,
        )
        if k:
            product = acc[slot, side] + product
        acc[slot, side] = product

    def reduce_tokens(slot, source):
        token_count = seg_v.shape[1]
        sequence = lax.broadcasted_iota(jnp.int32, (SUBLANES, token_count), 0)
        member = (sequence == seg_v[...]).astype(jnp.float32)
        part[source] = jnp.dot(
            member, acc[slot, 0] * acc[slot, 1],
            precision=lax.Precision.HIGHEST, preferred_element_type=jnp.float32,
        )

    for load in loads:
        load.wait()
    behind = None
    for n, (s, i) in enumerate(steps):
        if n < len(chunks):
            if n == 0 or chunks[n][0] != chunks[n - 1][0]:
                near[chunks[n][0]].wait_recv()
            project(0, chip, n)
            if n == len(chunks) - 1:
                reduce_tokens(0, chip)
        crossing[n].wait_recv()
        passing[n].start()
        if n + ahead < len(steps):
            crossing[n].wait_send()
            crossing[n + ahead].start()
        if behind is not None:
            passing[n - 1].wait_recv()
            project(1, origins[behind[0]], behind[1])
            if behind[1] == len(chunks) - 1:
                reduce_tokens(1, origins[behind[0]])
        behind = (s, i)
    passing[-1].wait_recv()
    project(1, origins[behind[0]], behind[1])
    reduce_tokens(1, origins[behind[0]])

    def sum_copy(d):
        target = lax.rem(layer + d, layers)
        return pltpu.make_async_remote_copy(
            src_ref=part.at[lax.div(target * query_lanes, LANES)], dst_ref=inbox.at[d - 1],
            send_sem=sum_send.at[d - 1], recv_sem=sum_recv.at[d - 1],
            device_id=others[d - 1], device_id_type=MESH,
        )

    summing = [sum_copy(d) for d in range(1, layers)]
    for copy in summing:
        copy.start()
    first = layer * query_lanes
    total = part[lax.div(first, LANES)]
    for n in range(len(steps)):
        if n + ahead >= len(steps):
            crossing[n].wait_send()
        passing[n].wait_send()
    for copy in near:
        copy.wait_send()
    for d in range(layers - 1):
        summing[d].wait_recv()
        total = total + inbox[d]
    query = lax.div(lax.broadcasted_iota(jnp.int32, total.shape, 1), RANK)
    first_query = lax.div(lax.rem(first, LANES), RANK)
    for j in range(query_lanes // RANK):
        score = jnp.sum(jnp.where(query == first_query + j, total, 0.0), axis=1, keepdims=True)
        out[:, j:j + 1] = score[:out.shape[0]]
    for copy in summing:
        copy.wait_send()


def local(mesh, activations, gradients, left_factors, right_factors, lengths, segment_ids):
    layers, chips = mesh.shape["layer"], mesh.shape["dp"] // 2
    rows, inner = left_factors.shape[1:]
    width = right_factors.shape[2]
    token_count, seq_count = segment_ids.shape[0], lengths.shape[0]
    query_lanes = 2 * chips * rows // layers
    chunks = chunks_of(inner, width, CHUNK if chips == 2 else 2048)
    hbm = pl.BlockSpec(memory_space=pl.ANY)
    dma = pltpu.SemaphoreType.DMA
    steps = (chips - 1, len(chunks))
    summed = pl.pallas_call(
        functools.partial(kernel, chunks, layers, chips, query_lanes),
        out_shape=jax.ShapeDtypeStruct((seq_count, query_lanes // RANK), jnp.float32),
        in_specs=[hbm] * 5,
        out_specs=pl.BlockSpec(memory_space=pltpu.VMEM),
        scratch_shapes=[
            pltpu.VMEM((token_count, inner), jnp.bfloat16),
            pltpu.VMEM((token_count, width), jnp.bfloat16),
            pltpu.VMEM((chips, 2 * rows, inner), jnp.bfloat16),
            pltpu.VMEM((chips, 2 * rows, width), jnp.bfloat16),
            pltpu.VMEM((1, token_count), jnp.int32),
            pltpu.VMEM((2, 2, token_count, 2 * rows), jnp.float32),
            pltpu.VMEM((chips, SUBLANES, 2 * rows), jnp.float32),
            pltpu.VMEM((layers - 1, SUBLANES, 2 * rows), jnp.float32),
            dma((5,)), dma((2,)), dma((2,)),
            dma(steps), dma(steps), dma(steps), dma(steps),
            dma((layers - 1,)), dma((layers - 1,)),
        ],
        compiler_params=pltpu.CompilerParams(
            collective_id=0, has_side_effects=True, vmem_limit_bytes=56 * 2**20
        ),
    )(activations, gradients, left_factors, right_factors, segment_ids.reshape(1, -1))
    return summed / lengths.astype(jnp.float32)[:, None]


def solution(mesh):
    return jax.shard_map(
        functools.partial(local, mesh),
        mesh=mesh,
        in_specs=(
            P("layer", ("groups", "dp"), None),
            P("layer", ("groups", "dp"), None),
            P("layer", ("groups", "dp"), None),
            P("layer", ("groups", "dp"), None),
            P(("groups", "dp")),
            P(("groups", "dp")),
        ),
        out_specs=P(("groups", "dp"), "layer"),
        check_vma=False,
    )
```

time: 93.9 us -> 48.7 us (0.52)
  waiting for transfers between devices: 54.2 us -> 0 us
  Pallas kernels: 0 us -> 46.4 us
  between operations: 14.1 us -> 0.01 us
  blocking collectives: 11.7 us -> 0 us
  matrix products: 11.2 us -> 0 us
    all_gather x2 -> x0, waiting for transfers between devices: 52.8 us -> none  [the longest x1 35.6 us: local(): left_piece = lax.all_gather(left_factors, 'dp', axis=1, tiled=True)]
    pallas_call x0 -> x1, Pallas kernels: none -> 46.4 us  [local(): pl.pallas_call(functools.partial(kernel, chunks, layers, chips, query_lan...]
    unnamed x1 -> x0, blocking collectives: 11.7 us -> none
    dot_general x3 -> x0, matrix products: 11.2 us -> none  [the longest x1 6.93 us: local(): lax.dot_general(activations[0], left_piece[0], (((1,), (1,)), ((), ())),...]
    unnamed x2 -> x0, waiting for transfers between devices: 1.41 us -> none
    unnamed x3 -> x0, local copies, waits for them, and re-layouts: 1.24 us -> none
  transfers between devices with their start and end apart: 2 -> 0, of which waited for: 2 -> 0; matrix products, arithmetic and copies ran while one was open for 9% -> 0% of each run, Pallas kernels for 0% -> 0%
where the time goes in v1:
time: 48.7 us; the launch traced here: 48.5 us
  Pallas kernels  46.4 us (95%)
  other arithmetic  1.41 us (3%)
  local copies, waits for them, and re-layouts  0.65 us (1%)
    pallas_call x1, Pallas kernels, local(): pl.pallas_call(functools.partial(kernel, chunks, layers, chips, query_lan...  46.4 us

profile of v1, /device:TPU:0, one launch (start us, length us, event | category | flops | bytes accessed | tf_op | source)
XLA Modules:
  0.0 48.5 jit_solution(16625899523628125000)
XLA Ops:
  0.0 0.7 %convert_element_type.3 = f32[4]{0:T(128)S(1)} convert(s32[4]{0:T(128)} %param.10) | non-fusion elementwise | flops 4 | bytes 32 | tf_op jit(solution)/shard_map/convert_element_type | solution.py:202
  0.7 46.4 %shard_map.64 = f32[4,2]{1,0:T(4,128)} custom-call(bf16[1,512,8192]{2,1,0:T(8,128)(2,1)} %act.1, bf16[1,512,4096]{2,1,0:T(8,128)(2,1)} %grad.1, bf16[1,64,8192]{2,1,0:T(8,128)(2,1)} %left.1, bf16[1,64,4096]{2,1,0:T(8,128)(2,1)} %right.1, s32[1,512]{1,0:T(1,128)} %bitcast.1), custom_call_target="tpu_custom_call" | custom-call | tf_op jit(solution)/shard_map/pallas_call | solution.py:180
  47.1 0.8 %broadcast_divide_fusion = f32[4,2]{1,0:T(4,128)S(1)} fusion(f32[4,2]{1,0:T(4,128)} %shard_map.64, f32[4]{0:T(128)S(1)} %convert_element_type.3), kind=kLoop, calls=%fused_computation | loop fusion | flops 8 | bytes 80 | tf_op jit(solution)/shard_map/div | solution.py:202
  47.8 0.7 %copy.7 = f32[4,2]{0,1:T(2,128)} copy(f32[4,2]{1,0:T(4,128)S(1)} %broadcast_divide_fusion) | data formatting | bytes 64 | tf_op jit(solution)/shard_map/div | solution.py:202

commit v2 on v1

--- a/solution.py
+++ b/solution.py
@@ -10,22 +10,24 @@
 RANK = 32
 LANES = 128
 SUBLANES = 8
-CHUNK = 512
+CHUNK = 1024
+TAPER = ()
 WINDOW = 0
 MESH = pl.DeviceIdType.MESH
 
 
-def chunks_of(inner, width, chunk):
+def chunks_of(inner, width, chunk, taper):
     left = [(0, k, chunk) for k in range(0, inner, chunk)]
-    right = [(1, k, chunk) for k in range(0, width, chunk)]
-    return left + right
+    right = [(1, k, chunk) for k in range(0, width - sum(taper), chunk)]
+    last = [(1, width - sum(taper[n:]), size) for n, size in enumerate(taper)]
+    return left + right + last
 
 
 def kernel(
     chunks, layers, chips, query_lanes,
-    act, grad, left, right, seg,
+    act, grad, left, right, seg, length,
     out,
-    act_v, grad_v, left_v, right_v, seg_v, acc, part, inbox,
+    act_v, grad_v, left_v, right_v, seg_v, length_s, acc, part, inbox,
     load_sem, near_send, near_recv, cross_send, cross_recv, pass_send, pass_recv,
     sum_send, sum_recv,
 ):
@@ -42,7 +44,7 @@
     others = [{"layer": lax.rem(layer + d, layers)} for d in range(1, layers)]
 
     barrier = pltpu.get_barrier_semaphore()
-    peers = [sibling] + partners + others
+    peers = others + partners + [sibling]
     for peer in peers:
         pl.semaphore_signal(barrier, inc=1, device_id=peer, device_id_type=MESH)
 
@@ -52,6 +54,7 @@
         pltpu.make_async_copy(act.at[0], act_v, load_sem.at[2]),
         pltpu.make_async_copy(grad.at[0], grad_v, load_sem.at[3]),
         pltpu.make_async_copy(seg, seg_v, load_sem.at[4]),
+        pltpu.make_async_copy(length, length_s, load_sem.at[5]),
     ]
     for load in loads:
         load.start()
@@ -147,6 +150,12 @@
     summing = [sum_copy(d) for d in range(1, layers)]
     for copy in summing:
         copy.start()
+    row = lax.broadcasted_iota(jnp.int32, part.shape[1:], 0)
+    lane = lax.broadcasted_iota(jnp.int32, part.shape[1:], 1)
+    count = jnp.ones((1, LANES), jnp.int32)
+    for g in range(out.shape[1]):
+        count = jnp.where(lane[:1] == g, length_s[g], count)
+    count = count.astype(jnp.float32)
     first = layer * query_lanes
     total = part[lax.div(first, LANES)]
     for n in range(len(steps)):
@@ -158,11 +167,12 @@
     for d in range(layers - 1):
         summing[d].wait_recv()
         total = total + inbox[d]
-    query = lax.div(lax.broadcasted_iota(jnp.int32, total.shape, 1), RANK)
+    query = lax.div(lane, RANK)
     first_query = lax.div(lax.rem(first, LANES), RANK)
     for j in range(query_lanes // RANK):
         score = jnp.sum(jnp.where(query == first_query + j, total, 0.0), axis=1, keepdims=True)
-        out[:, j:j + 1] = score[:out.shape[0]]
+        score = jnp.sum(jnp.where(row == lane, score, 0.0), axis=0, keepdims=True)
+        out[j:j + 1, :] = (score / count)[:, :out.shape[1]]
     for copy in summing:
         copy.wait_send()
 
@@ -173,14 +183,14 @@
     width = right_factors.shape[2]
     token_count, seq_count = segment_ids.shape[0], lengths.shape[0]
     query_lanes = 2 * chips * rows // layers
-    chunks = chunks_of(inner, width, CHUNK if chips == 2 else 2048)
+    chunks = chunks_of(inner, width, *((CHUNK, TAPER) if chips == 2 else (2048, ())))
     hbm = pl.BlockSpec(memory_space=pl.ANY)
     dma = pltpu.SemaphoreType.DMA
     steps = (chips - 1, len(chunks))
-    summed = pl.pallas_call(
+    scores = pl.pallas_call(
         functools.partial(kernel, chunks, layers, chips, query_lanes),
-        out_shape=jax.ShapeDtypeStruct((seq_count, query_lanes // RANK), jnp.float32),
-        in_specs=[hbm] * 5,
+        out_shape=jax.ShapeDtypeStruct((query_lanes // RANK, seq_count), jnp.float32),
+        in_specs=[hbm] * 6,
         out_specs=pl.BlockSpec(memory_space=pltpu.VMEM),
         scratch_shapes=[
             pltpu.VMEM((token_count, inner), jnp.bfloat16),
@@ -188,18 +198,19 @@
             pltpu.VMEM((chips, 2 * rows, inner), jnp.bfloat16),
             pltpu.VMEM((chips, 2 * rows, width), jnp.bfloat16),
             pltpu.VMEM((1, token_count), jnp.int32),
+            pltpu.SMEM((seq_count,), jnp.int32),
             pltpu.VMEM((2, 2, token_count, 2 * rows), jnp.float32),
             pltpu.VMEM((chips, SUBLANES, 2 * rows), jnp.float32),
             pltpu.VMEM((layers - 1, SUBLANES, 2 * rows), jnp.float32),
-            dma((5,)), dma((2,)), dma((2,)),
+            dma((6,)), dma((2,)), dma((2,)),
             dma(steps), dma(steps), dma(steps), dma(steps),
             dma((layers - 1,)), dma((layers - 1,)),
         ],
         compiler_params=pltpu.CompilerParams(
             collective_id=0, has_side_effects=True, vmem_limit_bytes=56 * 2**20
         ),
-    )(activations, gradients, left_factors, right_factors, segment_ids.reshape(1, -1))
-    return summed / lengths.astype(jnp.float32)[:, None]
+    )(activations, gradients, left_factors, right_factors, segment_ids.reshape(1, -1), lengths)
+    return scores.T
 
 
 def solution(mesh):

time: 48.7 us -> 47.6 us (0.977)
  other arithmetic: 1.41 us -> 0 us
  local copies, waits for them, and re-layouts: 0.65 us -> 1.24 us
    unnamed x0 -> x1, local copies, waits for them, and re-layouts: none -> 1.24 us
    div x1 -> x0, other arithmetic: 0.75 us -> none  [local(): return summed / lengths.astype(jnp.float32)[:, None]]
    convert_element_type x1 -> x0, other arithmetic: 0.66 us -> none  [local(): return summed / lengths.astype(jnp.float32)[:, None]]
    div x1 -> x0, local copies, waits for them, and re-layouts: 0.65 us -> none  [local(): return summed / lengths.astype(jnp.float32)[:, None]]
where the time goes in v2:
time: 47.6 us; the launch traced here: 47.4 us
  Pallas kernels  46.2 us (97%)
  local copies, waits for them, and re-layouts  1.24 us (3%)
    pallas_call x1, Pallas kernels, local(): pl.pallas_call(functools.partial(kernel, chunks, layers, chips, query_lan...  46.2 us
    unnamed x1, local copies, waits for them, and re-layouts  1.24 us

profile of v2, /device:TPU:0, one launch (start us, length us, event | category | flops | bytes accessed | tf_op | source)
XLA Modules:
  0.0 47.4 jit_solution(14519639637661906918)
XLA Ops:
  0.0 46.2 %shard_map.64 = f32[2,4]{1,0:T(2,128)} custom-call(bf16[1,512,8192]{2,1,0:T(8,128)(2,1)} %act.1, bf16[1,512,4096]{2,1,0:T(8,128)(2,1)} %grad.1, bf16[1,64,8192]{2,1,0:T(8,128)(2,1)} %left.1, bf16[1,64,4096]{2,1,0:T(8,128)(2,1)} %right.1, s32[1,512]{1,0:T(1,128)} %bitcast.3, s32[4]{0:T(128)} %length.1), custom_call_target="tpu_custom_call" | custom-call | tf_op jit(solution)/shard_map/pallas_call | solution.py:190
  46.2 1.2 %copy.8 = f32[4,2]{0,1:T(2,128)} copy(f32[4,2]{0,1:T(2,128)} %bitcast.2) | data formatting | bytes 64

commit v3 on v2

--- a/solution.py
+++ b/solution.py
@@ -108,11 +108,13 @@
     def reduce_tokens(slot, source):
         token_count = seg_v.shape[1]
         sequence = lax.broadcasted_iota(jnp.int32, (SUBLANES, token_count), 0)
-        member = (sequence == seg_v[...]).astype(jnp.float32)
-        part[source] = jnp.dot(
-            member, acc[slot, 0] * acc[slot, 1],
-            precision=lax.Precision.HIGHEST, preferred_element_type=jnp.float32,
-        )
+        member = (sequence == seg_v[...]).astype(jnp.bfloat16)
+        rest, total = acc[slot, 0] * acc[slot, 1], 0.0
+        for _ in range(3):
+            piece = rest.astype(jnp.bfloat16)
+            rest = rest - piece.astype(jnp.float32)
+            total += jnp.dot(member, piece, preferred_element_type=jnp.float32)
+        part[source] = total
 
     for load in loads:
         load.wait()

time: 47.6 us -> 47.5 us (level)
  no operation moved by 1% of the time
where the time goes in v3:
time: 47.5 us; the launch traced here: 47.4 us
  Pallas kernels  46.1 us (97%)
  local copies, waits for them, and re-layouts  1.24 us (3%)
    pallas_call x1, Pallas kernels, local(): pl.pallas_call(functools.partial(kernel, chunks, layers, chips, query_lan...  46.1 us
    unnamed x1, local copies, waits for them, and re-layouts  1.24 us

profile of v3, /device:TPU:0, one launch (start us, length us, event | category | flops | bytes accessed | tf_op | source)
XLA Modules:
  0.0 47.4 jit_solution(7280545636917806753)
XLA Ops:
  0.0 46.1 %shard_map.64 = f32[2,4]{1,0:T(2,128)} custom-call(bf16[1,512,8192]{2,1,0:T(8,128)(2,1)} %act.1, bf16[1,512,4096]{2,1,0:T(8,128)(2,1)} %grad.1, bf16[1,64,8192]{2,1,0:T(8,128)(2,1)} %left.1, bf16[1,64,4096]{2,1,0:T(8,128)(2,1)} %right.1, s32[1,512]{1,0:T(1,128)} %bitcast.3, s32[4]{0:T(128)} %length.1), custom_call_target="tpu_custom_call" | custom-call | tf_op jit(solution)/shard_map/pallas_call | solution.py:192
  46.2 1.2 %copy.8 = f32[4,2]{0,1:T(2,128)} copy(f32[4,2]{0,1:T(2,128)} %bitcast.2) | data formatting | bytes 64
